TPU v7x, 32 devices: a whole 2x2x4 slice. The times are simulated.
32 devices in a mesh: row: 8 (over y, x, core), col: 4 (over z).
Axes of the slice: x: 2, y: 2, z: 4, core: 2. Of those that a mesh axis runs over, the one named last changes fastest.
Arguments:
- blocks: float32 [8, 4, 288, 4096], P('row', 'col')
- block_slot: int32 [8, 4, 288], P('row', 'col'), may hold values from 0 to 73727, as said below
- sign_vec: int32 [98304], P(('col', 'row')), may hold values from -1 to 1, as said below
Outputs:
- normed_image: float32 [98304, 64], P(('col', 'row'))
- power_image: float32 [98304, 64], P(('col', 'row'))
Inputs may be any that keep to these rules, and one draw needn't show every extreme that they name: `block_slot`: each entry is i * 192 + j for a local block row i and block column j; the entries of one device are distinct, and each device names slot 0 and the last slot. `sign_vec`: every entry is -1 or 1.
All inputs are finite; a program needn't handle non-finite values.
Results may differ from a plain program's by a relative error of at most 0.0001.
Values sent between devices are 32-bit elements; how exact they have to be, the bound alone decides.
A program may use at most 128 MiB of HBM per device.

v0:
```python
import jax
import jax.numpy as jnp
from jax import lax
from jax.sharding import PartitionSpec as P

BLOCK = 64
PROBES = 64


def hadamard_sign(row_ids, probe_count):
    low_bits = row_ids % 128
    probe_ids = jnp.arange(probe_count, dtype=jnp.int32)
    parity = jnp.zeros((row_ids.shape[0], probe_count), jnp.int32)
    for bit_pos in range(7):
        left_bit = jnp.bitwise_and(jnp.right_shift(low_bits, bit_pos), 1)
        right_bit = jnp.bitwise_and(jnp.right_shift(probe_ids, bit_pos), 1)
        parity = parity + left_bit[:, None] * right_bit[None, :]
    return (1 - 2 * (parity % 2)).astype(jnp.float32)


def block_products(tiles, field, sources, targets, target_count, transpose):
    probe_count = field.shape[1]
    picked = field.reshape(-1, BLOCK, probe_count)[sources]
    pattern_text = "bji,bjk->bik" if transpose else "bij,bjk->bik"
    products = jnp.einsum(pattern_text, tiles, picked, precision=lax.Precision.HIGHEST)
    one_hot = (targets[None, :] == jnp.arange(target_count, dtype=jnp.int32)[:, None]).astype(
        jnp.float32
    )
    summed = jnp.dot(
        one_hot,
        products.reshape(tiles.shape[0], BLOCK * probe_count),
        precision=lax.Precision.HIGHEST,
        preferred_element_type=jnp.float32,
    )
    return summed.reshape(target_count * BLOCK, probe_count)


def local(blocks, block_slot, sign_vec):
    local_rows = sign_vec.shape[0]
    n_rows_axis = lax.axis_size("row")
    n_cols_axis = lax.axis_size("col")
    total_rows = local_rows * n_rows_axis * n_cols_axis
    band_rows = total_rows // n_cols_axis
    row_blocks = band_rows // BLOCK
    col_blocks = total_rows // n_rows_axis // BLOCK
    row_index = lax.axis_index("row")
    col_index = lax.axis_index("col")
    tiles = blocks.reshape(-1, BLOCK, BLOCK)
    slots = block_slot.reshape(-1)
    blk_row = slots // col_blocks
    blk_col = slots % col_blocks
    own_ids = (
        col_index * band_rows + row_index * local_rows + jnp.arange(local_rows, dtype=jnp.int32)
    )
    own_panel = sign_vec.astype(jnp.float32)[:, None] * hadamard_sign(own_ids, PROBES)
    panel = lax.all_gather(own_panel, "col", axis=0, tiled=True)
    partial_value = block_products(tiles, panel, blk_col, blk_row, row_blocks, False)
    first_own = lax.psum_scatter(partial_value, "row", scatter_dimension=0, tiled=True)
    col_sums = lax.psum(jnp.sum(first_own * first_own, axis=0), ("row", "col"))
    normed_own = first_own / jnp.sqrt(col_sums / total_rows + 1e-06)
    normed_col_band = lax.all_gather(normed_own, "row", axis=0, tiled=True)
    second_partial = block_products(tiles, normed_col_band, blk_row, blk_col, col_blocks, True)
    power_own = lax.psum_scatter(second_partial, "col", scatter_dimension=0, tiled=True)
    return (normed_own, power_own)


def solution(mesh):
    in_specs = (P("row", "col", None, None), P("row", "col", None), P(("col", "row")))
    out_specs = (P(("col", "row"), None), P(("col", "row"), None))
    return jax.shard_map(local, mesh=mesh, in_specs=in_specs, out_specs=out_specs, check_vma=False)
```

profile of v0, /device:TPU:0, one launch (start us, length us, event | category | flops | bytes accessed | tf_op | source)
XLA Modules:
  0.0 573.4 jit_solution(14866779846421602721)
XLA Ops:
  7.2 0.0 all-gather.3.cloned.1.call-start
  7.3 0.7 convert_element_type.8
  8.1 4.6 fusion.4
  12.7 0.0 all-gather.3.cloned.1.call-update
  12.7 0.0 reduce-scatter.3.cloned.1.call-start
  12.7 6.2 %copy.7 = f32[1,1,288,4096]{2,3,1,0:T(8,128)} copy(f32[1,1,288,4096]{3,2,1,0:T(8,128)} %param.3) | data formatting | bytes 9437184 | tf_op args[0]
  19.0 0.0 copy-start.2
  19.0 12.3 %copy.9 = f32[288,64,64]{2,1,0:T(8,128)} copy(f32[288,64,64]{0,2,1:T(8,128)} %bitcast.32) | data formatting | bytes 9437184 | tf_op jit(solution)/shard_map/reshape | solution.py:48
  31.2 0.0 copy-done.2
  31.4 99.5 %all-gather.3.cloned.1.call-done = f32[12288,64]{1,0:T(8,128)} async-done(((f32[3072,64]{1,0:T(8,128)}), f32[12288,64]{1,0:T(8,128)}) %all-gather.3.cloned.1.call-update) | async-done | bytes 3145744 | tf_op jit(solution)/shard_map/all_gather | solution.py:56
  130.9 7.6 %gather_fusion = f32[288,64,64]{2,1,0:T(8,128)} fusion(f32[192,64,64]{2,1,0:T(8,128)} %bitcast.33, s32[1024]{0:T(1024)S(1)} %pad_clamp_fusion.1), kind=kCustom, calls=%fused_computation | custom fusion | bytes 9438336 | tf_op jit(solution)/shard_map/gather | solution.py:23
  138.5 21.5 %convolution_bitcast_fusion.1 = f32[288,64,64]{1,2,0:T(8,128)} fusion(f32[288,64,64]{2,1,0:T(8,128)} %gather_fusion, f32[288,64,64]{2,1,0:T(8,128)} %copy.9), kind=kOutput, calls=%fused_computation.3 | convolution fusion | flops 905969664 | bytes 14155776 | tf_op jit(solution)/shard_map/bij,bjk->bik/dot_general | solution.py:25
  159.9 11.7 %copy.10 = f32[288,64,64]{0,2,1:T(8,128)} copy(f32[288,64,64]{1,2,0:T(8,128)} %convolution_bitcast_fusion.1) | data formatting | bytes 9437184 | tf_op jit(solution)/shard_map/bij,bjk->bik/dot_general | solution.py:25
  171.6 12.3 %fusion.5 = f32[384,4096]{1,0:T(8,128)} fusion(f32[288,4096]{0,1:T(8,128)} %bitcast.31, s32[288]{0:T(512)S(1)} %get-tuple-element.9), kind=kOutput, calls=%fused_computation.15 | convolution fusion | flops 5435928576 | bytes 11011200 | tf_op jit(solution)/shard_map/dot_general | solution.py:29
  183.9 10.8 %reshape.223 = f32[24576,64]{1,0:T(8,128)} reshape(f32[384,4096]{1,0:T(8,128)} %fusion.5) | data formatting | bytes 12582912 | tf_op jit(solution)/shard_map/reshape | solution.py:35
  194.7 0.0 reduce-scatter.3.cloned.1.call-update
  194.7 0.0 all-gather.5.cloned.1.call-start
  194.8 90.7 %reduce-scatter.3.cloned.1.call-done = f32[3072,64]{1,0:T(8,128)} async-done(((f32[24576,64]{1,0:T(8,128)}), f32[3072,64]{1,0:T(8,128)}) %reduce-scatter.3.cloned.1.call-update) | async-done | bytes 786448 | tf_op jit(solution)/shard_map/reduce_scatter | solution.py:58
  285.5 0.0 copy-start.1
  285.5 1.9 multiply_reduce_fusion
  287.4 39.3 %psum.7 = f32[64]{0:T(128)S(1)} all-reduce(f32[64]{0:T(128)S(1)} %multiply_reduce_fusion), channel_id=1, replica_groups=mesh['row'=8,'col'=4] {'row','col'}, use_global_device_ids=true, to_apply=%region_2.3 | all-reduce | flops 64 | bytes 512 | tf_op jit(solution)/shard_map/psum | solution.py:59
  326.8 0.0 copy-done.1
  326.8 1.3 broadcast_divide_fusion
  328.1 0.0 all-gather.5.cloned.1.call-update
  328.1 0.0 reduce-scatter.5.cloned.1.call-start
  328.2 72.7 %all-gather.5.cloned.1.call-done = f32[24576,64]{1,0:T(8,128)} async-done(((f32[3072,64]{1,0:T(8,128)}), f32[24576,64]{1,0:T(8,128)}) %all-gather.5.cloned.1.call-update) | async-done | bytes 6291472 | tf_op jit(solution)/shard_map/all_gather | solution.py:61
  400.9 9.4 %gather_fusion.1 = f32[288,64,64]{2,1,0:T(8,128)} fusion(f32[384,64,64]{2,1,0:T(8,128)} %bitcast.34, s32[1024]{0:T(1024)S(1)} %pad_clamp_fusion), kind=kCustom, calls=%fused_computation.1 | custom fusion | bytes 9438336 | tf_op jit(solution)/shard_map/gather | solution.py:23
  410.3 21.1 %convolution_bitcast_fusion = f32[288,64,64]{1,2,0:T(8,128)} fusion(f32[288,64,64]{2,1,0:T(8,128)} %gather_fusion.1, f32[288,64,64]{2,1,0:T(8,128)} %copy.9), kind=kOutput, calls=%fused_computation.2 | convolution fusion | flops 905969664 | bytes 14155776 | tf_op jit(solution)/shard_map/bji,bjk->bik/dot_general | solution.py:25
  431.4 11.6 %copy.15 = f32[288,64,64]{0,2,1:T(8,128)} copy(f32[288,64,64]{1,2,0:T(8,128)} %convolution_bitcast_fusion) | data formatting | bytes 9437184 | tf_op jit(solution)/shard_map/bji,bjk->bik/dot_general | solution.py:25
  443.0 5.9 %fusion.7 = f32[192,4096]{1,0:T(8,128)S(1)} fusion(f32[288,4096]{0,1:T(8,128)} %bitcast.30, s32[288]{0:T(512)S(1)} %get-tuple-element.8), kind=kOutput, calls=%fused_computation.18 | convolution fusion | flops 2717964288 | bytes 7865472 | tf_op jit(solution)/shard_map/dot_general | solution.py:29
  448.9 4.2 reshape.226
  453.2 0.0 copy-start
  453.2 0.0 reduce-scatter.5.cloned.1.call-update
  453.2 1.4 copy-done
  454.6 1.3 copy.16
  455.9 108.2 %reduce-scatter.5.cloned.1.call-done = f32[3072,64]{1,0:T(8,128)} async-done(((f32[12288,64]{1,0:T(8,128)}), f32[3072,64]{1,0:T(8,128)}) %reduce-scatter.5.cloned.1.call-update) | async-done | bytes 786448 | tf_op jit(solution)/shard_map/reduce_scatter | solution.py:63
  564.1 2.7 copy.17
  (15 shorter events, 0.2 us)
Async XLA Ops:
  7.2 123.7 %all-gather.3.cloned.1.call-start = ((), (), s32[]{:S(2)}) async-start(), calls=%async_computation.2 | async-start | bytes 7864320 | tf_op jit(solution)/shard_map/all_gather | solution.py:56
  12.7 272.8 %reduce-scatter.3.cloned.1.call-start = ((), (), s32[]{:S(2)}) async-start(), calls=%async_computation.3 | async-start | bytes 14155776 | tf_op jit(solution)/shard_map/reduce_scatter | solution.py:58
  19.0 12.3 %copy-start.2 = (s32[1,1,288]{2,1,0:T(1,128)S(1)}, s32[1,1,288]{2,1,0:T(1,128)}, u32[]{:S(2)}) copy-start(s32[1,1,288]{2,1,0:T(1,128)} %param.4) | copy-start | bytes 3460
  194.7 206.2 %all-gather.5.cloned.1.call-start = ((), (), s32[]{:S(2)}) async-start(), calls=%async_computation.4 | async-start | bytes 14155776 | tf_op jit(solution)/shard_map/all_gather | solution.py:61
  285.5 41.3 %copy-start.1 = (f32[3072,64]{1,0:T(8,128)S(1)}, f32[3072,64]{1,0:T(8,128)}, u32[]{:S(2)}) copy-start(f32[3072,64]{1,0:T(8,128)} %reduce-scatter.3.cloned.1.call-done) | copy-start | bytes 2359300
  328.1 236.0 %reduce-scatter.5.cloned.1.call-start = ((), (), s32[]{:S(2)}) async-start(), calls=%async_computation.5 | async-start | bytes 7864320 | tf_op jit(solution)/shard_map/reduce_scatter | solution.py:63
  453.2 1.4 copy-start
Sparse Core Ops, SparseCore 0:
  12.8 118.0 all-gather.2
  194.8 90.6 reduce-scatter.2
  328.2 72.6 all-gather.4
  453.3 110.7 reduce-scatter.4
where the time goes:
time: 574 us; the launch traced here: 573 us
  waiting for transfers between devices  371 us (65%)
  local copies, waits for them, and re-layouts  79.3 us (14%)
  matrix products  60.8 us (11%)
  blocking collectives  39.3 us (7%)
  between operations  13.9 us (2%)
  other arithmetic  8.73 us (2%)
    reduce_scatter x1, waiting for transfers between devices, local(): lax.psum_scatter(second_partial, 'col', scatter_dimension=0, tiled=True)  108 us
    all_gather x1, waiting for transfers between devices, local(): panel = lax.all_gather(own_panel, 'col', axis=0, tiled=True)  99.5 us
    reduce_scatter x1, waiting for transfers between devices, local(): lax.psum_scatter(partial_value, 'row', scatter_dimension=0, tiled=True)  90.7 us
    all_gather x1, waiting for transfers between devices, local(): normed_col_band = lax.all_gather(normed_own, 'row', axis=0, tiled=True)  72.7 us
    dot_general x2, matrix products, block_products(): jnp.einsum(pattern_text, tiles, picked, precision=lax.Precision.HIGHEST)  42.6 us
    psum x1, blocking collectives, local(): col_sums = lax.psum(jnp.sum(first_own * first_own, axis=0), ('row', 'col'))  39.3 us
    dot_general x2, local copies, waits for them, and re-layouts, block_products(): jnp.einsum(pattern_text, tiles, picked, precision=lax.Precision.HIGHEST)  23.2 us
    dot_general x2, matrix products, block_products(): jnp.dot(one_hot, products.reshape(tiles.shape[0], BLOCK * probe_count), p...  18.2 us
  transfers between devices with their start and end apart: 4, of which 4 were waited for; matrix products, arithmetic and copies ran while one was open for 3% of the time, Pallas kernels for 0%

commit v1 on v0

--- a/solution.py
+++ b/solution.py
@@ -56,7 +56,9 @@
     panel = lax.all_gather(own_panel, "col", axis=0, tiled=True)
     partial_value = block_products(tiles, panel, blk_col, blk_row, row_blocks, False)
     first_own = lax.psum_scatter(partial_value, "row", scatter_dimension=0, tiled=True)
-    col_sums = lax.psum(jnp.sum(first_own * first_own, axis=0), ("row", "col"))
+    col_sums = jnp.sum(first_own * first_own, axis=0)
+    for axis in ("col", "row"):
+        col_sums = lax.psum(col_sums, axis)
     normed_own = first_own / jnp.sqrt(col_sums / total_rows + 1e-06)
     normed_col_band = lax.all_gather(normed_own, "row", axis=0, tiled=True)
     second_partial = block_products(tiles, normed_col_band, blk_row, blk_col, col_blocks, True)

time: 574 us -> 555 us (0.967)
  blocking collectives: 39.3 us -> 23.5 us
    psum x1 -> x2, blocking collectives: 39.3 us -> 23.5 us  [local(): col_sums = lax.psum(col_sums, axis)]
  transfers between devices with their start and end apart: 4 -> 4, of which waited for: 4 -> 4; matrix products, arithmetic and copies ran while one was open for 3% -> 4% of each run, Pallas kernels for 0% -> 0%
where the time goes in v1:
time: 555 us; the launch traced here: 554 us
  waiting for transfers between devices  368 us (66%)
  local copies, waits for them, and re-layouts  79.3 us (14%)
  matrix products  60.8 us (11%)
  blocking collectives  23.5 us (4%)
  between operations  13.9 us (3%)
  other arithmetic  8.74 us (2%)
    reduce_scatter x1, waiting for transfers between devices, local(): lax.psum_scatter(second_partial, 'col', scatter_dimension=0, tiled=True)  108 us
    all_gather x1, waiting for transfers between devices, local(): panel = lax.all_gather(own_panel, 'col', axis=0, tiled=True)  99.5 us
    reduce_scatter x1, waiting for transfers between devices, local(): lax.psum_scatter(partial_value, 'row', scatter_dimension=0, tiled=True)  90.7 us
    all_gather x1, waiting for transfers between devices, local(): normed_col_band = lax.all_gather(normed_own, 'row', axis=0, tiled=True)  69.3 us
    dot_general x2, matrix products, block_products(): jnp.einsum(pattern_text, tiles, picked, precision=lax.Precision.HIGHEST)  42.6 us
    psum x2, blocking collectives, local(): col_sums = lax.psum(col_sums, axis)  23.5 us
    dot_general x2, local copies, waits for them, and re-layouts, block_products(): jnp.einsum(pattern_text, tiles, picked, precision=lax.Precision.HIGHEST)  23.2 us
    dot_general x2, matrix products, block_products(): jnp.dot(one_hot, products.reshape(tiles.shape[0], BLOCK * probe_count), p...  18.2 us
  transfers between devices with their start and end apart: 4, of which 4 were waited for; matrix products, arithmetic and copies ran while one was open for 4% of the time, Pallas kernels for 0%

profile of v1, /device:TPU:0, one launch (start us, length us, event | category | flops | bytes accessed | tf_op | source)
XLA Modules:
  0.0 554.1 jit_solution(6257303504813455373)
XLA Ops:
  7.2 0.0 all-gather.3.cloned.1.call-start
  7.3 0.7 convert_element_type.8
  8.1 4.6 fusion.4
  12.7 0.0 all-gather.3.cloned.1.call-update
  12.7 0.0 reduce-scatter.3.cloned.1.call-start
  12.7 6.2 %copy.7 = f32[1,1,288,4096]{2,3,1,0:T(8,128)} copy(f32[1,1,288,4096]{3,2,1,0:T(8,128)} %param.3) | data formatting | bytes 9437184 | tf_op args[0]
  19.0 0.0 copy-start.2
  19.0 12.3 %copy.9 = f32[288,64,64]{2,1,0:T(8,128)} copy(f32[288,64,64]{0,2,1:T(8,128)} %bitcast.32) | data formatting | bytes 9437184 | tf_op jit(solution)/shard_map/reshape | solution.py:48
  31.2 0.0 copy-done.2
  31.4 99.5 %all-gather.3.cloned.1.call-done = f32[12288,64]{1,0:T(8,128)} async-done(((f32[3072,64]{1,0:T(8,128)}), f32[12288,64]{1,0:T(8,128)}) %all-gather.3.cloned.1.call-update) | async-done | bytes 3145744 | tf_op jit(solution)/shard_map/all_gather | solution.py:56
  130.9 7.6 %gather_fusion = f32[288,64,64]{2,1,0:T(8,128)} fusion(f32[192,64,64]{2,1,0:T(8,128)} %bitcast.33, s32[1024]{0:T(1024)S(1)} %pad_clamp_fusion.1), kind=kCustom, calls=%fused_computation | custom fusion | bytes 9438336 | tf_op jit(solution)/shard_map/gather | solution.py:23
  138.5 21.5 %convolution_bitcast_fusion.1 = f32[288,64,64]{1,2,0:T(8,128)} fusion(f32[288,64,64]{2,1,0:T(8,128)} %gather_fusion, f32[288,64,64]{2,1,0:T(8,128)} %copy.9), kind=kOutput, calls=%fused_computation.3 | convolution fusion | flops 905969664 | bytes 14155776 | tf_op jit(solution)/shard_map/bij,bjk->bik/dot_general | solution.py:25
  159.9 11.7 %copy.10 = f32[288,64,64]{0,2,1:T(8,128)} copy(f32[288,64,64]{1,2,0:T(8,128)} %convolution_bitcast_fusion.1) | data formatting | bytes 9437184 | tf_op jit(solution)/shard_map/bij,bjk->bik/dot_general | solution.py:25
  171.6 12.3 %fusion.5 = f32[384,4096]{1,0:T(8,128)} fusion(f32[288,4096]{0,1:T(8,128)} %bitcast.31, s32[288]{0:T(512)S(1)} %get-tuple-element.9), kind=kOutput, calls=%fused_computation.15 | convolution fusion | flops 5435928576 | bytes 11011200 | tf_op jit(solution)/shard_map/dot_general | solution.py:29
  183.9 10.8 %reshape.223 = f32[24576,64]{1,0:T(8,128)} reshape(f32[384,4096]{1,0:T(8,128)} %fusion.5) | data formatting | bytes 12582912 | tf_op jit(solution)/shard_map/reshape | solution.py:35
  194.7 0.0 reduce-scatter.3.cloned.1.call-update
  194.7 0.0 all-gather.5.cloned.1.call-start
  194.8 90.7 %reduce-scatter.3.cloned.1.call-done = f32[3072,64]{1,0:T(8,128)} async-done(((f32[24576,64]{1,0:T(8,128)}), f32[3072,64]{1,0:T(8,128)}) %reduce-scatter.3.cloned.1.call-update) | async-done | bytes 786448 | tf_op jit(solution)/shard_map/reduce_scatter | solution.py:58
  285.5 0.0 copy-start.1
  285.5 1.9 multiply_reduce_fusion
  287.4 11.7 %psum.14 = f32[64]{0:T(128)S(1)} all-reduce(f32[64]{0:T(128)S(1)} %multiply_reduce_fusion), channel_id=1, replica_groups=mesh['row'=8,'col'=4] {'col'}, use_global_device_ids=true, to_apply=%region_2.3 | all-reduce | flops 64 | bytes 512 | tf_op jit(solution)/shard_map/psum | solution.py:61
  299.1 11.8 %psum.15 = f32[64]{0:T(128)S(1)} all-reduce(f32[64]{0:T(128)S(1)} %psum.14), channel_id=1, replica_groups=mesh['row'=8,'col'=4] {'row'}, use_global_device_ids=true, to_apply=%region_3.4 | all-reduce | flops 64 | bytes 512 | tf_op jit(solution)/shard_map/psum | solution.py:61
  310.9 0.0 copy-done.1
  310.9 1.3 broadcast_divide_fusion
  312.2 0.0 all-gather.5.cloned.1.call-update
  312.2 0.0 reduce-scatter.5.cloned.1.call-start
  312.3 69.3 %all-gather.5.cloned.1.call-done = f32[24576,64]{1,0:T(8,128)} async-done(((f32[3072,64]{1,0:T(8,128)}), f32[24576,64]{1,0:T(8,128)}) %all-gather.5.cloned.1.call-update) | async-done | bytes 6291472 | tf_op jit(solution)/shard_map/all_gather | solution.py:63
  381.6 9.4 %gather_fusion.1 = f32[288,64,64]{2,1,0:T(8,128)} fusion(f32[384,64,64]{2,1,0:T(8,128)} %bitcast.34, s32[1024]{0:T(1024)S(1)} %pad_clamp_fusion), kind=kCustom, calls=%fused_computation.1 | custom fusion | bytes 9438336 | tf_op jit(solution)/shard_map/gather | solution.py:23
  391.0 21.1 %convolution_bitcast_fusion = f32[288,64,64]{1,2,0:T(8,128)} fusion(f32[288,64,64]{2,1,0:T(8,128)} %gather_fusion.1, f32[288,64,64]{2,1,0:T(8,128)} %copy.9), kind=kOutput, calls=%fused_computation.2 | convolution fusion | flops 905969664 | bytes 14155776 | tf_op jit(solution)/shard_map/bji,bjk->bik/dot_general | solution.py:25
  412.1 11.6 %copy.15 = f32[288,64,64]{0,2,1:T(8,128)} copy(f32[288,64,64]{1,2,0:T(8,128)} %convolution_bitcast_fusion) | data formatting | bytes 9437184 | tf_op jit(solution)/shard_map/bji,bjk->bik/dot_general | solution.py:25
  423.7 5.9 %fusion.7 = f32[192,4096]{1,0:T(8,128)S(1)} fusion(f32[288,4096]{0,1:T(8,128)} %bitcast.30, s32[288]{0:T(512)S(1)} %get-tuple-element.8), kind=kOutput, calls=%fused_computation.18 | convolution fusion | flops 2717964288 | bytes 7865472 | tf_op jit(solution)/shard_map/dot_general | solution.py:29
  429.6 4.2 reshape.226
  433.9 0.0 copy-start
  433.9 0.0 reduce-scatter.5.cloned.1.call-update
  433.9 1.4 copy-done
  435.3 1.3 copy.16
  436.6 108.2 %reduce-scatter.5.cloned.1.call-done = f32[3072,64]{1,0:T(8,128)} async-done(((f32[12288,64]{1,0:T(8,128)}), f32[3072,64]{1,0:T(8,128)}) %reduce-scatter.5.cloned.1.call-update) | async-done | bytes 786448 | tf_op jit(solution)/shard_map/reduce_scatter | solution.py:65
  544.8 2.7 copy.17
  (15 shorter events, 0.2 us)
Async XLA Ops:
  7.2 123.7 %all-gather.3.cloned.1.call-start = ((), (), s32[]{:S(2)}) async-start(), calls=%async_computation.2 | async-start | bytes 7864320 | tf_op jit(solution)/shard_map/all_gather | solution.py:56
  12.7 272.8 %reduce-scatter.3.cloned.1.call-start = ((), (), s32[]{:S(2)}) async-start(), calls=%async_computation.3 | async-start | bytes 14155776 | tf_op jit(solution)/shard_map/reduce_scatter | solution.py:58
  19.0 12.3 %copy-start.2 = (s32[1,1,288]{2,1,0:T(1,128)S(1)}, s32[1,1,288]{2,1,0:T(1,128)}, u32[]{:S(2)}) copy-start(s32[1,1,288]{2,1,0:T(1,128)} %param.4) | copy-start | bytes 3460
  194.7 186.9 %all-gather.5.cloned.1.call-start = ((), (), s32[]{:S(2)}) async-start(), calls=%async_computation.4 | async-start | bytes 14155776 | tf_op jit(solution)/shard_map/all_gather | solution.py:63
  285.5 25.4 %copy-start.1 = (f32[3072,64]{1,0:T(8,128)S(1)}, f32[3072,64]{1,0:T(8,128)}, u32[]{:S(2)}) copy-start(f32[3072,64]{1,0:T(8,128)} %reduce-scatter.3.cloned.1.call-done) | copy-start | bytes 2359300
  312.2 232.6 %reduce-scatter.5.cloned.1.call-start = ((), (), s32[]{:S(2)}) async-start(), calls=%async_computation.5 | async-start | bytes 7864320 | tf_op jit(solution)/shard_map/reduce_scatter | solution.py:65
  433.9 1.4 copy-start
Sparse Core Ops, SparseCore 0:
  12.8 118.0 all-gather.2
  194.8 90.6 reduce-scatter.2
  312.4 69.2 all-gather.4
  434.0 110.7 reduce-scatter.4
